TPU v7x, 512 devices: a whole 4x8x8 slice. The times are simulated.
512 devices in a mesh: seq: 16 (over y, core), hid: 32 (over z, x).
Axes of the slice: x: 4, y: 8, z: 8, core: 2. Of those that a mesh axis runs over, the one named last changes fastest.
Arguments:
- query_stream: bfloat16 [12288, 8192], P('seq', 'hid'), may hold values from -6 to 6
- key_stream: bfloat16 [12288, 8192], P('seq', 'hid'), may hold values from -6 to 6
- value_stream: bfloat16 [12288, 8192], P('seq', 'hid'), may hold values from -6 to 6
- earlier_rows: bfloat16 [127, 8192], P(None, 'hid'), may hold values from -6 to 6
- filter_taps: float32 [8192, 128], P('hid'), may hold values from -0.4 to 0.4
- skip_gain: float32 [8192], P('hid'), may hold values from 0.5 to 1.5
- weight_values: bfloat16 [8192, 8192], P('seq', 'hid'), may hold values from -0.0625 to 0.0625
- weight_scales: float32 [64, 64], P('seq', 'hid'), may hold values from 0.5 to 2
Outputs:
- mixed_out: bfloat16 [12288, 8192], P('seq', 'hid')
All inputs are finite; a program needn't handle non-finite values.
Results may differ from a plain program's by a relative error of at most 0.0064.
Values may be sent and summed in bfloat16 or wider, within the bound.
A program may use at most 64 MiB of HBM per device.

v0:
```python
import jax
import jax.numpy as jnp
from jax import lax
from jax.sharding import PartitionSpec as P

BLOCK = 128


def from_behind(block, axis, distance):
    devices = range(lax.axis_size(axis))
    route = [(i - distance, i) for i in devices if i - distance in devices]
    return lax.ppermute(block, axis, route)


def causal_filter(signal, filter_taps):
    channels = signal.shape[1]
    kernel = jnp.transpose(filter_taps[:, ::-1])[:, None, :]
    result = lax.conv_general_dilated(
        signal[None],
        kernel,
        (1,),
        "VALID",
        dimension_numbers=("NWC", "WIO", "NWC"),
        feature_group_count=channels,
        precision=lax.Precision.HIGHEST,
    )
    return result[0]


def on_device(
    query_stream,
    key_stream,
    value_stream,
    earlier_rows,
    filter_taps,
    skip_gain,
    weight_values,
    weight_scales,
):
    margin = filter_taps.shape[1] - 1
    token_count = query_stream.shape[0]
    product = (key_stream.astype(jnp.float32) * value_stream.astype(jnp.float32)).astype(
        jnp.bfloat16
    )
    first_shard = lax.axis_index("seq") == 0
    arrived = from_behind(product[token_count - margin :], "seq", 1)
    preceding = jnp.where(first_shard, earlier_rows, arrived)
    extended = jnp.concatenate([preceding, product], axis=0).astype(jnp.float32)
    filtered = causal_filter(extended, filter_taps)
    filtered = filtered + skip_gain[None, :] * product.astype(jnp.float32)
    gated = (query_stream.astype(jnp.float32) * filtered).astype(jnp.bfloat16)
    spread = jnp.repeat(jnp.repeat(weight_scales, BLOCK, axis=0), BLOCK, axis=1)
    dequantized = (weight_values.astype(jnp.float32) * spread).astype(jnp.bfloat16)
    start_sum = jnp.zeros((token_count, weight_values.shape[1]), jnp.float32)
    panel = lax.all_gather(dequantized, "seq", axis=0, tiled=True)
    portion = lax.all_gather(gated, "hid", axis=1, tiled=True)
    weight_block = lax.slice_in_dim(panel, 0, portion.shape[1], axis=0)
    total = start_sum + jnp.dot(portion, weight_block, preferred_element_type=jnp.float32)
    return total.astype(jnp.bfloat16)


def solution(mesh):
    return jax.shard_map(
        on_device,
        mesh=mesh,
        in_specs=(
            P("seq", "hid"),
            P("seq", "hid"),
            P("seq", "hid"),
            P(None, "hid"),
            P("hid", None),
            P("hid"),
            P("seq", "hid"),
            P("seq", "hid"),
        ),
        out_specs=P("seq", "hid"),
        check_vma=False,
    )
```

profile of v0, /device:TPU:1, one launch (start us, length us, event | category | flops | bytes accessed | tf_op | source)
XLA Modules:
  0.0 209.6 jit_solution(14800829261201218460)
XLA Ops:
  6.5 0.0 all-gather.5.cloned.1.call-start
  6.5 0.8 copy.13
  7.3 0.6 broadcast_in_dim.16
  7.9 1.7 fusion.4
  9.6 0.0 all-gather.5.cloned.1.call-update
  9.7 0.0 all-gather.3.cloned.1.call-start
  9.7 1.2 multiply_convert_fusion
  11.0 4.6 %collective-permute-start = (bf16[127,256]{1,0:T(8,128)(2,1)S(1)}, bf16[127,256]{1,0:T(8,128)(2,1)S(1)}, u32[]{:S(2)}, u32[]{:S(2)}) collective-permute-start(bf16[127,256]{1,0:T(8,128)(2,1)S(1)} %slice.4), channel_id=1, source_target_pairs={{0,32},{32,64},{64,96},{96,128},{128,160},{160,192},{192,224},{224... | collective-permute-start | bytes 195080 | tf_op jit(solution)/shard_map/ppermute | solution.py:12
  15.6 1.0 rev.3
  16.6 0.1 copy.12
  16.7 3.2 %collective-permute-done = bf16[127,256]{1,0:T(8,128)(2,1)S(1)} collective-permute-done((bf16[127,256]{1,0:T(8,128)(2,1)S(1)}, bf16[127,256]{1,0:T(8,128)(2,1)S(1)}, u32[]{:S(2)}, u32[]{:S(2)}) %collective-permute-start) | collective-permute-done | bytes 65056 | tf_op jit(solution)/shard_map/ppermute | solution.py:12
  19.9 0.1 maximum_bitcast_fusion
  20.0 0.0 copy-start
  20.0 0.0 copy-start.1
  20.0 16.4 %fusion = f32[1,768,256]{2,0,1:T(1,128)S(1)} fusion(f32[128,1,256]{2,1,0:T(1,128)S(1)} %copy.12, bf16[1,895,256]{2,1,0:T(8,128)(2,1)S(1)} %maximum_bitcast_fusion), kind=kOutput, calls=%fused_computation.1 | convolution fusion | flops 301989888 | bytes 1375744 | tf_op jit(solution)/shard_map/conv_general_dilated | solution.py:18
  36.4 0.0 copy-done
  36.5 0.0 copy-done.1
  36.5 0.9 fusion.3
  37.4 0.0 all-gather.3.cloned.1.call-update
  37.4 22.9 %all-gather.5.cloned.1.call-done = bf16[8192,256]{1,0:T(8,128)(2,1)} async-done(((bf16[512,256]{1,0:T(8,128)(2,1)}), bf16[8192,256]{1,0:T(8,128)(2,1)}) %all-gather.5.cloned.1.call-update) | async-done | bytes 4194320 | tf_op jit(solution)/shard_map/all_gather | solution.py:55
  60.3 132.6 %all-gather.3.cloned.1.call-done = bf16[768,8192]{1,0:T(8,128)(2,1)} async-done(((bf16[768,256]{1,0:T(8,128)(2,1)}), bf16[768,8192]{1,0:T(8,128)(2,1)}) %all-gather.3.cloned.1.call-update) | async-done | bytes 12582928 | tf_op jit(solution)/shard_map/all_gather | solution.py:56
  192.8 9.9 %convolution_convert_fusion = bf16[768,256]{1,0:T(8,128)(2,1)} fusion(bf16[768,8192]{1,0:T(8,128)(2,1)} %all-gather.3.cloned.1.call-done, bf16[8192,256]{1,0:T(8,128)(2,1)} %all-gather.5.cloned.1.call-done), kind=kOutput, calls=%fused_computation | convolution fusion | flops 3221422080 | bytes 17170432 | tf_op jit(solution)/shard_map/dot_general | solution.py:58
  (3 shorter events, 0.1 us)
Async XLA Ops:
  6.5 53.7 %all-gather.5.cloned.1.call-start = ((), (), s32[]{:S(2)}) async-start(), calls=%async_computation.1 | async-start | bytes 4456448 | tf_op jit(solution)/shard_map/all_gather | solution.py:55
  9.7 183.2 %all-gather.3.cloned.1.call-start = ((), (), s32[]{:S(2)}) async-start(), calls=%async_computation | async-start | bytes 12976128 | tf_op jit(solution)/shard_map/all_gather | solution.py:56
  11.0 8.9 %collective-permute-start = (bf16[127,256]{1,0:T(8,128)(2,1)S(1)}, bf16[127,256]{1,0:T(8,128)(2,1)S(1)}, u32[]{:S(2)}, u32[]{:S(2)}) collective-permute-start(bf16[127,256]{1,0:T(8,128)(2,1)S(1)} %slice.4), channel_id=1, source_target_pairs={{0,32},{32,64},{64,96},{96,128},{128,160},{160,192},{192,224},{224... | collective-permute-start | bytes 195080 | tf_op jit(solution)/shard_map/ppermute | solution.py:12
  20.0 16.5 %copy-start = (bf16[768,256]{1,0:T(8,128)(2,1)S(1)}, bf16[768,256]{1,0:T(8,128)(2,1)}, u32[]{:S(2)}) copy-start(bf16[768,256]{1,0:T(8,128)(2,1)} %param.8) | copy-start | bytes 1179652
  20.0 16.5 %copy-start.1 = (f32[256]{0:T(256)S(1)}, f32[256]{0:T(256)}, u32[]{:S(2)}) copy-start(f32[256]{0:T(256)} %param.13) | copy-start | bytes 3076
Sparse Core Ops, SparseCore 0:
  9.8 50.4 all-gather.4
  63.3 129.4 all-gather.2
where the time goes:
time: 211 us; the launch traced here: 210 us
  waiting for transfers between devices  159 us (75%)
  matrix products  26.4 us (13%)
  between operations  13.5 us (6%)
  starting transfers between devices  4.64 us (2%)
  other arithmetic  3.92 us (2%)
  local copies, waits for them, and re-layouts  2.54 us (1%)
    all_gather x1, waiting for transfers between devices, on_device(): portion = lax.all_gather(gated, 'hid', axis=1, tiled=True)  133 us
    all_gather x1, waiting for transfers between devices, on_device(): panel = lax.all_gather(dequantized, 'seq', axis=0, tiled=True)  22.9 us
    conv_general_dilated x1, matrix products, causal_filter(): lax.conv_general_dilated(signal[None], kernel, (1,), 'VALID', dimension_n...  16.4 us
    dot_general x1, matrix products, on_device(): jnp.dot(portion, weight_block, preferred_element_type=jnp.float32)  9.92 us
    ppermute x1, starting transfers between devices, from_behind(): return lax.ppermute(block, axis, route)  4.59 us
  transfers between devices with their start and end apart: 3, of which 3 were waited for; matrix products, arithmetic and copies ran while one was open for 9% of the time, Pallas kernels for 0%

commit v1 on v0

v1 whole, which is shorter than its diff:
```python
import functools

import jax
import jax.numpy as jnp
from jax import lax
from jax.experimental import pallas as pl
from jax.experimental.pallas import tpu as pltpu
from jax.sharding import PartitionSpec as P

MESH = pl.DeviceIdType.MESH
X = 4
CORES = 2
BLOCK = 128
LANES = 128
SUB = 8
ROWS = 128


def hops(n, even):
    far = n // 2
    return (far, n - 1 - far) if even else (n - 1 - far, far)


def kernel(
    ny,
    nz,
    q_hbm,
    k_hbm,
    v_hbm,
    e_hbm,
    t_hbm,
    g_hbm,
    w_hbm,
    s_ref,
    o_hbm,
    q_v,
    k_v,
    v_v,
    e_v,
    t_v,
    g_v,
    w_v,
    halo_out,
    halo_in,
    ext,
    taps,
    deq,
    a_buf,
    b_buf,
    c_send,
    c_recv,
    own,
    o_v,
    in_sem,
    halo_sem,
    a_send_sem,
    a_recv_sem,
    b_send_sem,
    b_recv_sem,
    m_send_sem,
    m_recv_sem,
    t_send_sem,
    t_recv_sem,
    c_send_sem,
    c_recv_sem,
    o_sem,
):
    tokens, width = q_v.shape
    chunks = tokens // ROWS
    half = ROWS
    s, hid = lax.axis_index("seq"), lax.axis_index("hid")
    y, c = s // CORES, s % CORES
    z, x = hid // X, hid % X

    def at(y_, c_, z_, x_):
        return (y_ * CORES + c_, z_ * X + x_)

    z_up, z_down = at(y, c, (z + 1) % nz, x), at(y, c, (z + nz - 1) % nz, x)
    y_up, y_down = at((y + 1) % ny, c, z, x), at((y + ny - 1) % ny, c, z, x)
    sibling = at(y, 1 - c, z, x)
    seq_next = ((s + 1) % (ny * CORES), hid)

    loads = [
        pltpu.make_async_copy(src, dst, in_sem.at[n])
        for n, (src, dst) in enumerate(
            (
                (w_hbm, w_v),
                (k_hbm, k_v),
                (v_hbm, v_v),
                (t_hbm, t_v),
                (g_hbm, g_v),
                (q_hbm, q_v),
                (e_hbm, e_v),
            )
        )
    ]
    for load in loads:
        load.start()

    barrier = pltpu.get_barrier_semaphore()
    partners = [
        at(y, (c + dc) % CORES, z, (x + dx) % X)
        for dc in range(CORES)
        for dx in range(X)
        if (dc, dx) != (0, 0)
    ]
    partners += [z_up, z_down, y_up, y_down]
    partners += [at((y + ny + 2 * c - 1) % ny, 1 - c, z, x)]
    for partner in partners:
        pl.semaphore_signal(barrier, inc=1, device_id=partner, device_id_type=MESH)

    loads[0].wait()
    for i in range(w_v.shape[0] // BLOCK):
        for n in range(width // BLOCK):
            rows, cols = pl.ds(i * BLOCK, BLOCK), pl.ds(n * BLOCK, BLOCK)
            deq[rows, cols] = (
                w_v[rows, cols].astype(jnp.float32) * s_ref[i, n]
            ).astype(jnp.bfloat16)

    loads[1].wait()
    loads[2].wait()
    for i in range(chunks):
        rows = pl.ds(i * ROWS, ROWS)
        product = (
            k_v[rows, :].astype(jnp.float32) * v_v[rows, :].astype(jnp.float32)
        ).astype(jnp.bfloat16)
        if i == chunks - 1:
            halo_out[...] = product
        wide = product.astype(jnp.float32)
        for n in range(width // LANES):
            ext[n, pl.ds(ROWS + i * ROWS, ROWS), :] = wide[:, n * LANES : (n + 1) * LANES]

    pl.semaphore_wait(barrier, len(partners))

    def turn(e, core):
        here = (x == 2 * c + e) & (c == core)
        src = deq.at[pl.ds((2 * e + core) * half, half), :]
        dst = b_buf.at[x, pl.ds(pl.multiple_of((2 * y + core) * half, half), half), :]
        remote = pltpu.make_async_remote_copy(
            src_ref=src,
            dst_ref=dst,
            send_sem=t_send_sem.at[e, core],
            recv_sem=t_recv_sem.at[x],
            device_id=at(y, core, z, 2 * c + e),
            device_id_type=MESH,
        )
        local = pltpu.make_async_copy(src, dst, t_recv_sem.at[x])
        return here, remote, local

    turns = [turn(e, core) for e in range(2) for core in range(CORES)]
    for here, remote, local in turns:
        pl.when(jnp.logical_not(here))(remote.start)
        pl.when(here)(local.start)

    halo = pltpu.make_async_remote_copy(
        src_ref=halo_out,
        dst_ref=halo_in,
        send_sem=halo_sem.at[0],
        recv_sem=halo_sem.at[1],
        device_id=seq_next,
        device_id_type=MESH,
    )
    halo.start()

    loads[3].wait()
    loads[4].wait()
    for n in range(width // LANES):
        flat = t_v[n * LANES : (n + 1) * LANES, :].T
        taps[n] = jnp.broadcast_to(flat[:, None, :], taps.shape[1:])
        taps[n, 0] = taps[n, 0] + g_v[:, n * LANES : (n + 1) * LANES]

    loads[5].wait()

    order = [(i + 1) % chunks for i in range(chunks)]

    def preceding():
        loads[6].wait()
        halo.wait_recv()

        @pl.when(s == 0)
        def _():
            early = e_v[...].astype(jnp.float32)
            for n in range(width // LANES):
                ext[n, pl.ds(1, ROWS - 1), :] = early[:, n * LANES : (n + 1) * LANES]

        @pl.when(s != 0)
        def _():
            early = halo_in[...].astype(jnp.float32)
            for n in range(width // LANES):
                ext[n, pl.ds(0, ROWS), :] = early[:, n * LANES : (n + 1) * LANES]

    def filter_chunk(i):
        base = order[i] * ROWS
        tiles = ROWS // SUB
        reach = taps.shape[1] // SUB
        for n in range(width // LANES):

            def phase(b, sums):
                sums = list(sums)
                factor = [taps[n, a * SUB + b] for a in range(reach)]
                for d in range(1 - reach, tiles):
                    value = ext[n, pl.ds(ROWS + base + d * SUB - b, SUB), :]
                    for a in range(reach):
                        if 0 <= d + a < tiles:
                            sums[d + a] = sums[d + a] + factor[a] * value
                return tuple(sums)

            zero = jnp.zeros((SUB, LANES), jnp.float32)
            sums = lax.fori_loop(0, SUB, phase, (zero,) * tiles)
            filtered = jnp.concatenate(sums, axis=0)
            cols = pl.ds(n * LANES, LANES)
            a_buf[z, pl.ds(base, ROWS), cols] = (
                q_v[pl.ds(base, ROWS), cols].astype(jnp.float32) * filtered
            ).astype(jnp.bfloat16)

    def a_copy(i, way, hop):
        step = 1 if way == 0 else -1
        block = a_buf.at[(z + nz - step * hop) % nz, pl.ds(order[i] * ROWS, ROWS), :]
        return pltpu.make_async_remote_copy(
            src_ref=block,
            dst_ref=block,
            send_sem=a_send_sem,
            recv_sem=a_recv_sem.at[i, way, hop],
            device_id=z_up if way == 0 else z_down,
            device_id_type=MESH,
        )

    def a_arrived(i, way, hop):
        step = 1 if way == 0 else -1
        block = a_buf.at[
            (z + nz - step * (hop + 1)) % nz, pl.ds(order[i] * ROWS, ROWS), :
        ]
        pltpu.make_async_copy(block, block, a_recv_sem.at[i, way, hop]).wait()

    def a_forward(i, way, hop):
        a_arrived(i, way, hop)
        if hop + 1 < hops(nz, i % 2 == 0)[way]:
            a_copy(i, way, hop + 1).start()

    def piece_column(p):
        return (x + (2, 1, 3, 0)[p]) % X

    def b_block(p, owner, core):
        rows = pl.ds(pl.multiple_of((2 * owner + core) * half, half), half)
        return b_buf.at[piece_column(p), rows, :]

    def b_copy(p, way, hop):
        step = 1 if way == 0 else -1
        block = b_block(p, (y + ny - step * hop) % ny, c)
        return pltpu.make_async_remote_copy(
            src_ref=block,
            dst_ref=block,
            send_sem=b_send_sem,
            recv_sem=b_recv_sem.at[p, way, hop],
            device_id=y_up if way == 0 else y_down,
            device_id_type=MESH,
        )

    def to_sibling(p, owner):
        block = b_block(p, owner, c)
        pltpu.make_async_remote_copy(
            src_ref=block,
            dst_ref=block,
            send_sem=m_send_sem,
            recv_sem=m_recv_sem.at[p, owner],
            device_id=sibling,
            device_id_type=MESH,
        ).start()

    def b_start(p):
        column = piece_column(p)
        block = b_block(p, y, c)
        pltpu.make_async_copy(block, block, t_recv_sem.at[column]).wait()
        for way in range(2):
            if hops(ny, p % 2 == 0)[way]:
                b_copy(p, way, 0).start()
        to_sibling(p, y)

    def b_forward(p, way, hop):
        step = 1 if way == 0 else -1
        owner = (y + ny - step * (hop + 1)) % ny
        block = b_block(p, owner, c)
        pltpu.make_async_copy(block, block, b_recv_sem.at[p, way, hop]).wait()
        if hop + 1 < hops(ny, p % 2 == 0)[way]:
            b_copy(p, way, hop + 1).start()
        to_sibling(p, owner)

    def b_whole(p):
        for owner in range(ny):
            block = b_block(p, owner, 1 - c)
            pltpu.make_async_copy(block, block, m_recv_sem.at[p, owner]).wait()

    def multiply(i, p):
        rows = pl.ds(order[i] * ROWS, ROWS)
        left = jnp.concatenate([a_buf[k, rows, :] for k in range(nz)], axis=1)
        total = jnp.dot(
            left, b_buf[piece_column(p)], preferred_element_type=jnp.float32
        )
        if p == X - 1:
            own[rows, :] = total
            return
        c_send[p, rows, :] = total.astype(jnp.bfloat16)
        pltpu.make_async_remote_copy(
            src_ref=c_send.at[p, rows, :],
            dst_ref=c_recv.at[p, rows, :],
            send_sem=c_send_sem,
            recv_sem=c_recv_sem.at[i, p],
            device_id=at(y, c, z, piece_column(p)),
            device_id_type=MESH,
        ).start()

    def finish(i):
        rows = pl.ds(order[i] * ROWS, ROWS)
        total = own[rows, :]
        for p in range(X - 1):
            block = c_recv.at[p, rows, :]
            pltpu.make_async_copy(block, block, c_recv_sem.at[i, p]).wait()
            total = total + c_recv[p, rows, :].astype(jnp.float32)
        o_v[rows, :] = total.astype(jnp.bfloat16)
        pltpu.make_async_copy(o_v.at[rows, :], o_hbm.at[rows, :], o_sem).start()

    far_a, far_b = nz // 2, ny // 2
    last = max(chunks + far_a, X + far_b)
    todo = []
    ready = []
    for k in range(last):
        if k < chunks:
            if order[k] == 0:
                preceding()
            filter_chunk(k)
            for way in range(2):
                if hops(nz, k % 2 == 0)[way]:
                    a_copy(k, way, 0).start()
        if k < X:
            b_start(k)
        events = []
        for hop in reversed(range(max(far_a, far_b))):
            for way in range(2):
                i = k - 1 - hop
                if 0 <= i < chunks and hop < hops(nz, i % 2 == 0)[way]:
                    events.append(functools.partial(a_forward, i, way, hop))
                if 0 <= i < X and hop < hops(ny, i % 2 == 0)[way]:
                    events.append(functools.partial(b_forward, i, way, hop))
        share = -(-len(todo) // max(1, len(events)))
        for event in events:
            event()
            for work in todo[:share]:
                work()
            del todo[:share]
        for work in todo:
            work()
        todo = []
        p = k - far_b
        if 0 <= p < X:
            todo.append(functools.partial(b_whole, p))
            todo += [
                functools.partial(multiply, i, p)
                for i in range(min(chunks, max(0, k - far_a)))
            ]
        i = k - far_a
        if 0 <= i < chunks:
            todo += [
                functools.partial(multiply, i, p)
                for p in range(min(X, k - far_b + 1))
            ]
        for i in ready:
            todo.append(functools.partial(finish, i))
        ready = []
        if k - far_b >= X - 1:
            done = min(chunks, k - far_a + 1)
            first = 0 if k - far_b == X - 1 else max(0, k - far_a)
            ready = list(range(first, done))
    for work in todo:
        work()
    for i in ready:
        finish(i)

    for here, remote, local in turns:
        pl.when(jnp.logical_not(here))(remote.wait_send)
    halo.wait_send()
    sent = a_buf.at[pl.ds(0, nz - 1)]
    pltpu.make_async_copy(sent, sent, a_send_sem).wait()
    sent = b_buf.at[:, pl.ds(0, (ny - 1) * half), :]
    pltpu.make_async_copy(sent, sent, b_send_sem).wait()
    sent = b_buf.at[:, pl.ds(0, ny * half), :]
    pltpu.make_async_copy(sent, sent, m_send_sem).wait()
    pltpu.make_async_copy(c_send, c_send, c_send_sem).wait()
    pltpu.make_async_copy(o_v, o_v, o_sem).wait()


def on_device(ny, nz, q, k, v, earlier, taps, gain, weight, scales):
    tokens, width = q.shape
    depth = weight.shape[0]
    reach = taps.shape[1]
    chunks = tokens // ROWS
    vmem, dma = pltpu.VMEM, pltpu.SemaphoreType.DMA
    bf16, f32 = jnp.bfloat16, jnp.float32
    anywhere = pl.BlockSpec(memory_space=pl.ANY)
    gain = gain.reshape(1, width)
    return pl.pallas_call(
        functools.partial(kernel, ny, nz),
        out_shape=jax.ShapeDtypeStruct((tokens, width), bf16),
        in_specs=[anywhere] * 7 + [pl.BlockSpec(memory_space=pltpu.SMEM)],
        out_specs=anywhere,
        scratch_shapes=[
            vmem(q.shape, bf16),
            vmem(k.shape, bf16),
            vmem(v.shape, bf16),
            vmem(earlier.shape, bf16),
            vmem(taps.shape, f32),
            vmem(gain.shape, f32),
            vmem(weight.shape, bf16),
            vmem((ROWS, width), bf16),
            vmem((ROWS, width), bf16),
            vmem((width // LANES, ROWS + tokens, LANES), f32),
            vmem((width // LANES, reach, SUB, LANES), f32),
            vmem((depth, width), bf16),
            vmem((nz, tokens, width), bf16),
            vmem((X, nz * width, width), bf16),
            vmem((X - 1, tokens, width), bf16),
            vmem((X - 1, tokens, width), bf16),
            vmem((tokens, width), f32),
            vmem((tokens, width), bf16),
            dma((7,)),
            dma((2,)),
            dma,
            dma((chunks, 2, nz // 2)),
            dma,
            dma((X, 2, ny // 2)),
            dma,
            dma((X, ny)),
            dma((2, CORES)),
            dma((X,)),
            dma,
            dma((chunks, X - 1)),
            dma,
        ],
        compiler_params=pltpu.CompilerParams(
            collective_id=0, has_side_effects=True, vmem_limit_bytes=40 * 1024 * 1024
        ),
        cost_estimate=pl.CostEstimate(
            flops=2 * tokens * nz * width * X * width,
            bytes_accessed=4 * tokens * width * 2,
            transcendentals=0,
        ),
    )(q, k, v, earlier, taps, gain, weight, scales)


def solution(mesh):
    ny = mesh.shape["seq"] // CORES
    nz = mesh.shape["hid"] // X
    return jax.shard_map(
        functools.partial(on_device, ny, nz),
        mesh=mesh,
        in_specs=(
            P("seq", "hid"),
            P("seq", "hid"),
            P("seq", "hid"),
            P(None, "hid"),
            P("hid", None),
            P("hid"),
            P("seq", "hid"),
            P("seq", "hid"),
        ),
        out_specs=P("seq", "hid"),
        check_vma=False,
    )
```

time: 211 us -> 77.6 us (0.37)
  the two profiles are of different devices: /device:TPU:1 before, /device:TPU:16 now
where the time goes in v1:
time: 77.6 us; the launch traced here: 77.3 us
  Pallas kernels  69.5 us (90%)
  local copies, waits for them, and re-layouts  7.78 us (10%)
    pallas_call x1, Pallas kernels, on_device(): pl.pallas_call(functools.partial(kernel, ny, nz), out_shape=jax.ShapeDtyp...  69.5 us
    unnamed x18, local copies, waits for them, and re-layouts  7.78 us

profile of v1, /device:TPU:16, one launch (start us, length us, event | category | flops | bytes accessed | tf_op | source)
XLA Modules:
  0.0 77.3 jit_solution(17369878540995976336)
XLA Ops:
  0.0 0.0 copy-start.7
  0.0 0.7 copy-done.7
  0.7 0.0 copy-start.6
  0.7 0.1 copy.9.s_ref
  0.8 0.6 copy-done.6
  1.4 0.0 copy-start
  1.4 1.0 %copy-done = bf16[768,256]{1,0:T(8,128)(2,1)S(1)} copy-done((bf16[768,256]{1,0:T(8,128)(2,1)S(1)}, bf16[768,256]{1,0:T(8,128)(2,1)}, u32[]{:S(2)}) %copy-start) | copy-done | bytes 393240
  2.4 0.0 copy-start.1
  2.4 1.0 %copy-done.1 = bf16[768,256]{1,0:T(8,128)(2,1)S(1)} copy-done((bf16[768,256]{1,0:T(8,128)(2,1)S(1)}, bf16[768,256]{1,0:T(8,128)(2,1)}, u32[]{:S(2)}) %copy-start.1) | copy-done | bytes 393240
  3.4 0.0 copy-start.2
  3.4 1.0 %copy-done.2 = bf16[768,256]{1,0:T(8,128)(2,1)S(1)} copy-done((bf16[768,256]{1,0:T(8,128)(2,1)S(1)}, bf16[768,256]{1,0:T(8,128)(2,1)}, u32[]{:S(2)}) %copy-start.2) | copy-done | bytes 393240
  4.3 0.0 copy-start.3
  4.4 0.9 %copy-done.3 = bf16[512,256]{1,0:T(8,128)(2,1)S(1)} copy-done((bf16[512,256]{1,0:T(8,128)(2,1)S(1)}, bf16[512,256]{1,0:T(8,128)(2,1)}, u32[]{:S(2)}) %copy-start.3) | copy-done | bytes 262168
  5.3 0.0 copy-start.4
  5.3 0.9 %copy-done.4 = f32[256,128]{1,0:T(8,128)S(1)} copy-done((f32[256,128]{1,0:T(8,128)S(1)}, f32[256,128]{1,0:T(8,128)}, u32[]{:S(2)}) %copy-start.4) | copy-done | bytes 131096
  6.2 0.0 copy-start.5
  6.2 0.8 %copy-done.5 = bf16[127,256]{1,0:T(8,128)(2,1)S(1)} copy-done((bf16[127,256]{1,0:T(8,128)(2,1)S(1)}, bf16[127,256]{1,0:T(8,128)(2,1)}, u32[]{:S(2)}) %copy-start.5) | copy-done | bytes 65048
  7.0 69.5 %shard_map.82 = bf16[768,256]{1,0:T(8,128)(2,1)S(1)} custom-call(bf16[768,256]{1,0:T(8,128)(2,1)S(1)} %copy-done, bf16[768,256]{1,0:T(8,128)(2,1)S(1)} %copy-done.1, bf16[768,256]{1,0:T(8,128)(2,1)S(1)} %copy-done.2, bf16[127,256]{1,0:T(8,128)(2,1)S(1)} %copy-done.5, f32[256,128]{1,0:T(8,128)S(1)} %copy-done.4, f32[1,256]{1,0:T(1,128)S(1)} %bitcast.1, ...), custom_call_target="tpu_custom_call" | custom-call | flops 3221225472 | bytes 1572864 | tf_op jit(solution)/shard_map/pallas_call | solution.py:400
  76.5 0.7 copy.11
Async XLA Ops:
  0.0 0.7 copy-start.7
  0.7 0.7 copy-start.6
  1.4 1.0 %copy-start = (bf16[768,256]{1,0:T(8,128)(2,1)S(1)}, bf16[768,256]{1,0:T(8,128)(2,1)}, u32[]{:S(2)}) copy-start(bf16[768,256]{1,0:T(8,128)(2,1)} %q_hbm.1) | copy-start | bytes 1179652
  2.4 1.0 %copy-start.1 = (bf16[768,256]{1,0:T(8,128)(2,1)S(1)}, bf16[768,256]{1,0:T(8,128)(2,1)}, u32[]{:S(2)}) copy-start(bf16[768,256]{1,0:T(8,128)(2,1)} %k_hbm.1) | copy-start | bytes 1179652
  3.4 1.0 %copy-start.2 = (bf16[768,256]{1,0:T(8,128)(2,1)S(1)}, bf16[768,256]{1,0:T(8,128)(2,1)}, u32[]{:S(2)}) copy-start(bf16[768,256]{1,0:T(8,128)(2,1)} %v_hbm.1) | copy-start | bytes 1179652
  4.3 0.9 %copy-start.3 = (bf16[512,256]{1,0:T(8,128)(2,1)S(1)}, bf16[512,256]{1,0:T(8,128)(2,1)}, u32[]{:S(2)}) copy-start(bf16[512,256]{1,0:T(8,128)(2,1)} %w_hbm.1) | copy-start | bytes 786436
  5.3 0.9 %copy-start.4 = (f32[256,128]{1,0:T(8,128)S(1)}, f32[256,128]{1,0:T(8,128)}, u32[]{:S(2)}) copy-start(f32[256,128]{1,0:T(8,128)} %t_hbm.1) | copy-start | bytes 393220
  6.2 0.8 %copy-start.5 = (bf16[127,256]{1,0:T(8,128)(2,1)S(1)}, bf16[127,256]{1,0:T(8,128)(2,1)}, u32[]{:S(2)}) copy-start(bf16[127,256]{1,0:T(8,128)(2,1)} %e_hbm.1) | copy-start | bytes 195076

commit v2 on v1

--- a/solution.py
+++ b/solution.py
@@ -14,6 +14,31 @@
 LANES = 128
 SUB = 8
 ROWS = 128
+FILTER, A_BEGIN, A_FORWARD, B_BEGIN, B_FORWARD, B_WHOLE, MULTIPLY, FINISH = range(8)
+PLAN = (
+    (A_BEGIN, 0), (FILTER, 1), (B_BEGIN, 0), (A_BEGIN, 1), (FILTER, 2), (B_BEGIN, 1), (A_BEGIN, 2), (FILTER, 3),
+    (A_FORWARD, 0, 0, 0), (A_FORWARD, 0, 1, 0), (B_BEGIN, 2), (B_FORWARD, 0, 0, 0), (A_FORWARD, 1, 0, 0),
+    (A_FORWARD, 1, 1, 0), (B_FORWARD, 0, 1, 0), (FILTER, 4), (B_FORWARD, 1, 0, 0), (A_FORWARD, 2, 0, 0),
+    (A_FORWARD, 2, 1, 0), (B_FORWARD, 1, 1, 0), (FILTER, 5), (A_FORWARD, 0, 0, 1), (A_FORWARD, 0, 1, 1),
+    (B_FORWARD, 2, 0, 0), (B_FORWARD, 2, 1, 0), (A_FORWARD, 1, 0, 1), (A_FORWARD, 1, 1, 1), (B_FORWARD, 0, 0, 1),
+    (B_FORWARD, 0, 1, 1), (A_FORWARD, 2, 0, 1), (A_FORWARD, 2, 1, 1), (B_FORWARD, 1, 0, 1), (B_FORWARD, 1, 1, 1),
+    (A_FORWARD, 0, 0, 2), (A_FORWARD, 0, 1, 2), (B_FORWARD, 2, 0, 1), (B_FORWARD, 2, 1, 1), (A_BEGIN, 3),
+    (A_FORWARD, 1, 0, 2), (A_FORWARD, 1, 1, 2), (B_FORWARD, 0, 0, 2), (B_FORWARD, 0, 1, 2), (B_BEGIN, 3),
+    (A_FORWARD, 2, 0, 2), (A_FORWARD, 2, 1, 2), (B_FORWARD, 1, 0, 2), (B_FORWARD, 1, 1, 2), (A_BEGIN, 4),
+    (A_FORWARD, 0, 0, 3), (A_FORWARD, 3, 1, 0), (B_FORWARD, 2, 0, 2), (B_FORWARD, 2, 1, 2), (A_FORWARD, 1, 1, 3),
+    (A_FORWARD, 3, 0, 0), (B_FORWARD, 0, 0, 3), (B_FORWARD, 3, 1, 0), (A_BEGIN, 5), (A_FORWARD, 2, 0, 3),
+    (A_FORWARD, 4, 1, 0), (B_FORWARD, 1, 1, 3), (B_FORWARD, 3, 0, 0), (B_WHOLE, 0), (MULTIPLY, 0, 0),
+    (A_FORWARD, 3, 1, 1), (A_FORWARD, 4, 0, 0), (B_FORWARD, 2, 0, 3), (MULTIPLY, 1, 0), (MULTIPLY, 2, 0),
+    (B_FORWARD, 3, 1, 1), (B_WHOLE, 1), (MULTIPLY, 0, 1), (A_FORWARD, 3, 0, 1), (A_FORWARD, 5, 1, 0),
+    (MULTIPLY, 1, 1), (MULTIPLY, 2, 1), (B_FORWARD, 3, 0, 1), (B_WHOLE, 2), (MULTIPLY, 0, 2), (A_FORWARD, 4, 1, 1),
+    (A_FORWARD, 5, 0, 0), (MULTIPLY, 1, 2), (MULTIPLY, 2, 2), (A_FORWARD, 3, 1, 2), (A_FORWARD, 4, 0, 1),
+    (B_FORWARD, 3, 1, 2), (B_FORWARD, 3, 0, 2), (A_FORWARD, 3, 0, 2), (A_FORWARD, 5, 1, 1), (A_FORWARD, 4, 1, 2),
+    (A_FORWARD, 5, 0, 1), (B_FORWARD, 3, 1, 3), (A_FORWARD, 3, 1, 3), (A_FORWARD, 4, 0, 2), (MULTIPLY, 3, 0),
+    (MULTIPLY, 3, 1), (MULTIPLY, 3, 2), (A_FORWARD, 5, 1, 2), (B_WHOLE, 3), (MULTIPLY, 0, 3), (A_FORWARD, 5, 0, 2),
+    (MULTIPLY, 1, 3), (MULTIPLY, 2, 3), (MULTIPLY, 3, 3), (FINISH, 0), (A_FORWARD, 4, 0, 3), (MULTIPLY, 4, 0),
+    (MULTIPLY, 4, 1), (MULTIPLY, 4, 2), (MULTIPLY, 4, 3), (A_FORWARD, 5, 1, 3), (MULTIPLY, 5, 0), (MULTIPLY, 5, 1),
+    (MULTIPLY, 5, 2), (MULTIPLY, 5, 3), (FINISH, 1), (FINISH, 2), (FINISH, 3), (FINISH, 4), (FINISH, 5),
+)
 
 
 def hops(n, even):
@@ -32,7 +57,7 @@
     g_hbm,
     w_hbm,
     s_ref,
-    o_hbm,
+    o_ref,
     q_v,
     k_v,
     v_v,
@@ -50,7 +75,6 @@
     c_send,
     c_recv,
     own,
-    o_v,
     in_sem,
     halo_sem,
     a_send_sem,
@@ -63,7 +87,6 @@
     t_recv_sem,
     c_send_sem,
     c_recv_sem,
-    o_sem,
 ):
     tokens, width = q_v.shape
     chunks = tokens // ROWS
@@ -109,14 +132,6 @@
     for partner in partners:
         pl.semaphore_signal(barrier, inc=1, device_id=partner, device_id_type=MESH)
 
-    loads[0].wait()
-    for i in range(w_v.shape[0] // BLOCK):
-        for n in range(width // BLOCK):
-            rows, cols = pl.ds(i * BLOCK, BLOCK), pl.ds(n * BLOCK, BLOCK)
-            deq[rows, cols] = (
-                w_v[rows, cols].astype(jnp.float32) * s_ref[i, n]
-            ).astype(jnp.bfloat16)
-
     loads[1].wait()
     loads[2].wait()
     for i in range(chunks):
@@ -130,7 +145,20 @@
         for n in range(width // LANES):
             ext[n, pl.ds(ROWS + i * ROWS, ROWS), :] = wide[:, n * LANES : (n + 1) * LANES]
 
-    pl.semaphore_wait(barrier, len(partners))
+    loads[3].wait()
+    loads[4].wait()
+    for n in range(width // LANES):
+        flat = t_v[n * LANES : (n + 1) * LANES, :].T
+        taps[n] = jnp.broadcast_to(flat[:, None, :], taps.shape[1:])
+        taps[n, 0] = taps[n, 0] + g_v[:, n * LANES : (n + 1) * LANES]
+
+    loads[0].wait()
+    for i in range(w_v.shape[0] // BLOCK):
+        for n in range(width // BLOCK):
+            rows, cols = pl.ds(i * BLOCK, BLOCK), pl.ds(n * BLOCK, BLOCK)
+            deq[rows, cols] = (
+                w_v[rows, cols].astype(jnp.float32) * s_ref[n, i]
+            ).astype(jnp.bfloat16)
 
     def turn(e, core):
         here = (x == 2 * c + e) & (c == core)
@@ -148,10 +176,6 @@
         return here, remote, local
 
     turns = [turn(e, core) for e in range(2) for core in range(CORES)]
-    for here, remote, local in turns:
-        pl.when(jnp.logical_not(here))(remote.start)
-        pl.when(here)(local.start)
-
     halo = pltpu.make_async_remote_copy(
         src_ref=halo_out,
         dst_ref=halo_in,
@@ -160,17 +184,6 @@
         device_id=seq_next,
         device_id_type=MESH,
     )
-    halo.start()
-
-    loads[3].wait()
-    loads[4].wait()
-    for n in range(width // LANES):
-        flat = t_v[n * LANES : (n + 1) * LANES, :].T
-        taps[n] = jnp.broadcast_to(flat[:, None, :], taps.shape[1:])
-        taps[n, 0] = taps[n, 0] + g_v[:, n * LANES : (n + 1) * LANES]
-
-    loads[5].wait()
-
     order = [(i + 1) % chunks for i in range(chunks)]
 
     def preceding():
@@ -191,6 +204,8 @@
 
     def filter_chunk(i):
         base = order[i] * ROWS
+        if base == 0:
+            preceding()
         tiles = ROWS // SUB
         reach = taps.shape[1] // SUB
         for n in range(width // LANES):
@@ -212,6 +227,15 @@
             a_buf[z, pl.ds(base, ROWS), cols] = (
                 q_v[pl.ds(base, ROWS), cols].astype(jnp.float32) * filtered
             ).astype(jnp.bfloat16)
+
+    loads[5].wait()
+    filter_chunk(0)
+
+    pl.semaphore_wait(barrier, len(partners))
+    for here, remote, local in turns:
+        pl.when(jnp.logical_not(here))(remote.start)
+        pl.when(here)(local.start)
+    halo.start()
 
     def a_copy(i, way, hop):
         step = 1 if way == 0 else -1
@@ -316,64 +340,25 @@
             block = c_recv.at[p, rows, :]
             pltpu.make_async_copy(block, block, c_recv_sem.at[i, p]).wait()
             total = total + c_recv[p, rows, :].astype(jnp.float32)
-        o_v[rows, :] = total.astype(jnp.bfloat16)
-        pltpu.make_async_copy(o_v.at[rows, :], o_hbm.at[rows, :], o_sem).start()
-
-    far_a, far_b = nz // 2, ny // 2
-    last = max(chunks + far_a, X + far_b)
-    todo = []
-    ready = []
-    for k in range(last):
-        if k < chunks:
-            if order[k] == 0:
-                preceding()
-            filter_chunk(k)
-            for way in range(2):
-                if hops(nz, k % 2 == 0)[way]:
-                    a_copy(k, way, 0).start()
-        if k < X:
-            b_start(k)
-        events = []
-        for hop in reversed(range(max(far_a, far_b))):
-            for way in range(2):
-                i = k - 1 - hop
-                if 0 <= i < chunks and hop < hops(nz, i % 2 == 0)[way]:
-                    events.append(functools.partial(a_forward, i, way, hop))
-                if 0 <= i < X and hop < hops(ny, i % 2 == 0)[way]:
-                    events.append(functools.partial(b_forward, i, way, hop))
-        share = -(-len(todo) // max(1, len(events)))
-        for event in events:
-            event()
-            for work in todo[:share]:
-                work()
-            del todo[:share]
-        for work in todo:
-            work()
-        todo = []
-        p = k - far_b
-        if 0 <= p < X:
-            todo.append(functools.partial(b_whole, p))
-            todo += [
-                functools.partial(multiply, i, p)
-                for i in range(min(chunks, max(0, k - far_a)))
-            ]
-        i = k - far_a
-        if 0 <= i < chunks:
-            todo += [
-                functools.partial(multiply, i, p)
-                for p in range(min(X, k - far_b + 1))
-            ]
-        for i in ready:
-            todo.append(functools.partial(finish, i))
-        ready = []
-        if k - far_b >= X - 1:
-            done = min(chunks, k - far_a + 1)
-            first = 0 if k - far_b == X - 1 else max(0, k - far_a)
-            ready = list(range(first, done))
-    for work in todo:
-        work()
-    for i in ready:
-        finish(i)
+        o_ref[rows, :] = total.astype(jnp.bfloat16)
+
+    def a_begin(i):
+        for way in range(2):
+            if hops(nz, i % 2 == 0)[way]:
+                a_copy(i, way, 0).start()
+
+    work = {
+        FILTER: filter_chunk,
+        A_BEGIN: a_begin,
+        A_FORWARD: a_forward,
+        B_BEGIN: b_start,
+        B_FORWARD: b_forward,
+        B_WHOLE: b_whole,
+        MULTIPLY: multiply,
+        FINISH: finish,
+    }
+    for name, *where in PLAN:
+        work[name](*where)
 
     for here, remote, local in turns:
         pl.when(jnp.logical_not(here))(remote.wait_send)
@@ -385,7 +370,6 @@
     sent = b_buf.at[:, pl.ds(0, ny * half), :]
     pltpu.make_async_copy(sent, sent, m_send_sem).wait()
     pltpu.make_async_copy(c_send, c_send, c_send_sem).wait()
-    pltpu.make_async_copy(o_v, o_v, o_sem).wait()
 
 
 def on_device(ny, nz, q, k, v, earlier, taps, gain, weight, scales):
@@ -395,13 +379,13 @@
     chunks = tokens // ROWS
     vmem, dma = pltpu.VMEM, pltpu.SemaphoreType.DMA
     bf16, f32 = jnp.bfloat16, jnp.float32
-    anywhere = pl.BlockSpec(memory_space=pl.ANY)
+    anywhere = pl.BlockSpec(memory_space=pltpu.HBM)
     gain = gain.reshape(1, width)
     return pl.pallas_call(
         functools.partial(kernel, ny, nz),
         out_shape=jax.ShapeDtypeStruct((tokens, width), bf16),
         in_specs=[anywhere] * 7 + [pl.BlockSpec(memory_space=pltpu.SMEM)],
-        out_specs=anywhere,
+        out_specs=pl.BlockSpec(memory_space=pltpu.VMEM),
         scratch_shapes=[
             vmem(q.shape, bf16),
             vmem(k.shape, bf16),
@@ -420,7 +404,6 @@
             vmem((X - 1, tokens, width), bf16),
             vmem((X - 1, tokens, width), bf16),
             vmem((tokens, width), f32),
-            vmem((tokens, width), bf16),
             dma((7,)),
             dma((2,)),
             dma,
@@ -433,17 +416,16 @@
             dma((X,)),
             dma,
             dma((chunks, X - 1)),
-            dma,
         ],
         compiler_params=pltpu.CompilerParams(
-            collective_id=0, has_side_effects=True, vmem_limit_bytes=40 * 1024 * 1024
+            collective_id=0, has_side_effects=True, vmem_limit_bytes=63 * 1024 * 1024
         ),
         cost_estimate=pl.CostEstimate(
             flops=2 * tokens * nz * width * X * width,
             bytes_accessed=4 * tokens * width * 2,
             transcendentals=0,
         ),
-    )(q, k, v, earlier, taps, gain, weight, scales)
+    )(q, k, v, earlier, taps, gain, weight, scales.T)
 
 
 def solution(mesh):

time: 77.6 us -> 62 us (0.80)
  the two profiles are of different devices: /device:TPU:16 before, /device:TPU:1 now
where the time goes in v2:
time: 62 us; the launch traced here: 61.8 us
  Pallas kernels  60.1 us (97%)
  local copies, waits for them, and re-layouts  1.77 us (3%)
    pallas_call x1, Pallas kernels, on_device(): pl.pallas_call(functools.partial(kernel, ny, nz), out_shape=jax.ShapeDtyp...  60.1 us
    unnamed x1, local copies, waits for them, and re-layouts  1.77 us

profile of v2, /device:TPU:1, one launch (start us, length us, event | category | flops | bytes accessed | tf_op | source)
XLA Modules:
  0.0 61.8 jit_solution(10752548599668064880)
XLA Ops:
  0.0 60.1 %shard_map.82 = bf16[768,256]{1,0:T(8,128)(2,1)} custom-call(bf16[768,256]{1,0:T(8,128)(2,1)} %q_hbm.1, bf16[768,256]{1,0:T(8,128)(2,1)} %k_hbm.1, bf16[768,256]{1,0:T(8,128)(2,1)} %v_hbm.1, bf16[127,256]{1,0:T(8,128)(2,1)} %e_hbm.1, f32[256,128]{1,0:T(8,128)} %t_hbm.1, f32[1,256]{1,0:T(1,128)} %bitcast.2, bf16[512,256]{1,0:T(8,128)(2,1)} %w_hbm.1, ...), custom_call_target="tpu_custom_call" | custom-call | flops 3221225472 | bytes 1572864 | tf_op jit(solution)/shard_map/pallas_call | solution.py:384
  60.1 1.8 %copy.10 = bf16[768,256]{1,0:T(8,128)(2,1)} copy(bf16[768,256]{1,0:T(8,128)(2,1)} %shard_map.82) | data formatting | bytes 786432

commit v3 on v2

--- a/solution.py
+++ b/solution.py
@@ -103,6 +103,18 @@
     sibling = at(y, 1 - c, z, x)
     seq_next = ((s + 1) % (ny * CORES), hid)
 
+    barrier = pltpu.get_barrier_semaphore()
+    partners = [z_up, z_down, y_up, y_down]
+    partners += [
+        at(y, (c + dc) % CORES, z, (x + dx) % X)
+        for dc in range(CORES)
+        for dx in range(X)
+        if (dc, dx) != (0, 0)
+    ]
+    partners += [at((y + ny + 2 * c - 1) % ny, 1 - c, z, x)]
+    for partner in partners:
+        pl.semaphore_signal(barrier, inc=1, device_id=partner, device_id_type=MESH)
+
     loads = [
         pltpu.make_async_copy(src, dst, in_sem.at[n])
         for n, (src, dst) in enumerate(
@@ -120,38 +132,6 @@
     for load in loads:
         load.start()
 
-    barrier = pltpu.get_barrier_semaphore()
-    partners = [
-        at(y, (c + dc) % CORES, z, (x + dx) % X)
-        for dc in range(CORES)
-        for dx in range(X)
-        if (dc, dx) != (0, 0)
-    ]
-    partners += [z_up, z_down, y_up, y_down]
-    partners += [at((y + ny + 2 * c - 1) % ny, 1 - c, z, x)]
-    for partner in partners:
-        pl.semaphore_signal(barrier, inc=1, device_id=partner, device_id_type=MESH)
-
-    loads[1].wait()
-    loads[2].wait()
-    for i in range(chunks):
-        rows = pl.ds(i * ROWS, ROWS)
-        product = (
-            k_v[rows, :].astype(jnp.float32) * v_v[rows, :].astype(jnp.float32)
-        ).astype(jnp.bfloat16)
-        if i == chunks - 1:
-            halo_out[...] = product
-        wide = product.astype(jnp.float32)
-        for n in range(width // LANES):
-            ext[n, pl.ds(ROWS + i * ROWS, ROWS), :] = wide[:, n * LANES : (n + 1) * LANES]
-
-    loads[3].wait()
-    loads[4].wait()
-    for n in range(width // LANES):
-        flat = t_v[n * LANES : (n + 1) * LANES, :].T
-        taps[n] = jnp.broadcast_to(flat[:, None, :], taps.shape[1:])
-        taps[n, 0] = taps[n, 0] + g_v[:, n * LANES : (n + 1) * LANES]
-
     loads[0].wait()
     for i in range(w_v.shape[0] // BLOCK):
         for n in range(width // BLOCK):
@@ -176,6 +156,24 @@
         return here, remote, local
 
     turns = [turn(e, core) for e in range(2) for core in range(CORES)]
+    pl.semaphore_wait(barrier, len(partners))
+    for here, remote, local in turns:
+        pl.when(jnp.logical_not(here))(remote.start)
+        pl.when(here)(local.start)
+
+    loads[1].wait()
+    loads[2].wait()
+    for i in range(chunks):
+        rows = pl.ds(i * ROWS, ROWS)
+        product = (
+            k_v[rows, :].astype(jnp.float32) * v_v[rows, :].astype(jnp.float32)
+        ).astype(jnp.bfloat16)
+        if i == chunks - 1:
+            halo_out[...] = product
+        wide = product.astype(jnp.float32)
+        for n in range(width // LANES):
+            ext[n, pl.ds(ROWS + i * ROWS, ROWS), :] = wide[:, n * LANES : (n + 1) * LANES]
+
     halo = pltpu.make_async_remote_copy(
         src_ref=halo_out,
         dst_ref=halo_in,
@@ -184,6 +182,8 @@
         device_id=seq_next,
         device_id_type=MESH,
     )
+    halo.start()
+
     order = [(i + 1) % chunks for i in range(chunks)]
 
     def preceding():
@@ -228,14 +228,15 @@
                 q_v[pl.ds(base, ROWS), cols].astype(jnp.float32) * filtered
             ).astype(jnp.bfloat16)
 
+    loads[3].wait()
+    loads[4].wait()
+    for n in range(width // LANES):
+        flat = t_v[n * LANES : (n + 1) * LANES, :].T
+        taps[n] = jnp.broadcast_to(flat[:, None, :], taps.shape[1:])
+        taps[n, 0] = taps[n, 0] + g_v[:, n * LANES : (n + 1) * LANES]
+
     loads[5].wait()
     filter_chunk(0)
-
-    pl.semaphore_wait(barrier, len(partners))
-    for here, remote, local in turns:
-        pl.when(jnp.logical_not(here))(remote.start)
-        pl.when(here)(local.start)
-    halo.start()
 
     def a_copy(i, way, hop):
         step = 1 if way == 0 else -1
@@ -383,7 +384,7 @@
     gain = gain.reshape(1, width)
     return pl.pallas_call(
         functools.partial(kernel, ny, nz),
-        out_shape=jax.ShapeDtypeStruct((tokens, width), bf16),
+        out_shape=pltpu.VMEM((tokens, width), bf16),
         in_specs=[anywhere] * 7 + [pl.BlockSpec(memory_space=pltpu.SMEM)],
         out_specs=pl.BlockSpec(memory_space=pltpu.VMEM),
         scratch_shapes=[

time: 62 us -> 60.3 us (0.973)
  local copies, waits for them, and re-layouts: 1.77 us -> 0.75 us
  Pallas kernels: 60.1 us -> 59.4 us
    unnamed x1, local copies, waits for them, and re-layouts: 1.77 us -> 0.75 us
    pallas_call x1, Pallas kernels: 60.1 us -> 59.4 us  [on_device(): pl.pallas_call(functools.partial(kernel, ny, nz), out_shape=pltpu.VMEM((t...]
where the time goes in v3:
time: 60.3 us; the launch traced here: 60.2 us
  Pallas kernels  59.4 us (99%)
  local copies, waits for them, and re-layouts  0.75 us (1%)
    pallas_call x1, Pallas kernels, on_device(): pl.pallas_call(functools.partial(kernel, ny, nz), out_shape=pltpu.VMEM((t...  59.4 us

profile of v3, /device:TPU:1, one launch (start us, length us, event | category | flops | bytes accessed | tf_op | source)
XLA Modules:
  0.0 60.2 jit_solution(16520193822211628517)
XLA Ops:
  0.0 59.4 %shard_map.82 = bf16[768,256]{1,0:T(8,128)(2,1)S(1)} custom-call(bf16[768,256]{1,0:T(8,128)(2,1)} %q_hbm.1, bf16[768,256]{1,0:T(8,128)(2,1)} %k_hbm.1, bf16[768,256]{1,0:T(8,128)(2,1)} %v_hbm.1, bf16[127,256]{1,0:T(8,128)(2,1)} %e_hbm.1, f32[256,128]{1,0:T(8,128)} %t_hbm.1, f32[1,256]{1,0:T(1,128)} %bitcast.2, bf16[512,256]{1,0:T(8,128)(2,1)} %w_hbm.1, ...), custom_call_target="tpu_custom_call" | custom-call | flops 3221225472 | bytes 1572864 | tf_op jit(solution)/shard_map/pallas_call | solution.py:385
  59.4 0.7 %copy.10 = bf16[768,256]{1,0:T(8,128)(2,1)} copy(bf16[768,256]{1,0:T(8,128)(2,1)S(1)} %shard_map.82) | data formatting | bytes 786432

commit v4 on v3

--- a/solution.py
+++ b/solution.py
@@ -24,19 +24,19 @@
     (B_FORWARD, 0, 1, 1), (A_FORWARD, 2, 0, 1), (A_FORWARD, 2, 1, 1), (B_FORWARD, 1, 0, 1), (B_FORWARD, 1, 1, 1),
     (A_FORWARD, 0, 0, 2), (A_FORWARD, 0, 1, 2), (B_FORWARD, 2, 0, 1), (B_FORWARD, 2, 1, 1), (A_BEGIN, 3),
     (A_FORWARD, 1, 0, 2), (A_FORWARD, 1, 1, 2), (B_FORWARD, 0, 0, 2), (B_FORWARD, 0, 1, 2), (B_BEGIN, 3),
-    (A_FORWARD, 2, 0, 2), (A_FORWARD, 2, 1, 2), (B_FORWARD, 1, 0, 2), (B_FORWARD, 1, 1, 2), (A_BEGIN, 4),
+    (B_FORWARD, 1, 0, 2), (A_FORWARD, 2, 0, 2), (B_FORWARD, 1, 1, 2), (A_FORWARD, 2, 1, 2), (A_BEGIN, 4),
     (A_FORWARD, 0, 0, 3), (A_FORWARD, 3, 1, 0), (B_FORWARD, 2, 0, 2), (B_FORWARD, 2, 1, 2), (A_FORWARD, 1, 1, 3),
     (A_FORWARD, 3, 0, 0), (B_FORWARD, 0, 0, 3), (B_FORWARD, 3, 1, 0), (A_BEGIN, 5), (A_FORWARD, 2, 0, 3),
-    (A_FORWARD, 4, 1, 0), (B_FORWARD, 1, 1, 3), (B_FORWARD, 3, 0, 0), (B_WHOLE, 0), (MULTIPLY, 0, 0),
-    (A_FORWARD, 3, 1, 1), (A_FORWARD, 4, 0, 0), (B_FORWARD, 2, 0, 3), (MULTIPLY, 1, 0), (MULTIPLY, 2, 0),
+    (A_FORWARD, 4, 1, 0), (B_FORWARD, 1, 1, 3), (B_FORWARD, 2, 0, 3), (B_FORWARD, 3, 0, 0), (B_WHOLE, 0),
+    (MULTIPLY, 0, 0), (A_FORWARD, 3, 1, 1), (A_FORWARD, 4, 0, 0), (MULTIPLY, 1, 0), (MULTIPLY, 2, 0),
     (B_FORWARD, 3, 1, 1), (B_WHOLE, 1), (MULTIPLY, 0, 1), (A_FORWARD, 3, 0, 1), (A_FORWARD, 5, 1, 0),
     (MULTIPLY, 1, 1), (MULTIPLY, 2, 1), (B_FORWARD, 3, 0, 1), (B_WHOLE, 2), (MULTIPLY, 0, 2), (A_FORWARD, 4, 1, 1),
     (A_FORWARD, 5, 0, 0), (MULTIPLY, 1, 2), (MULTIPLY, 2, 2), (A_FORWARD, 3, 1, 2), (A_FORWARD, 4, 0, 1),
     (B_FORWARD, 3, 1, 2), (B_FORWARD, 3, 0, 2), (A_FORWARD, 3, 0, 2), (A_FORWARD, 5, 1, 1), (A_FORWARD, 4, 1, 2),
     (A_FORWARD, 5, 0, 1), (B_FORWARD, 3, 1, 3), (A_FORWARD, 3, 1, 3), (A_FORWARD, 4, 0, 2), (MULTIPLY, 3, 0),
     (MULTIPLY, 3, 1), (MULTIPLY, 3, 2), (A_FORWARD, 5, 1, 2), (B_WHOLE, 3), (MULTIPLY, 0, 3), (A_FORWARD, 5, 0, 2),
-    (MULTIPLY, 1, 3), (MULTIPLY, 2, 3), (MULTIPLY, 3, 3), (FINISH, 0), (A_FORWARD, 4, 0, 3), (MULTIPLY, 4, 0),
-    (MULTIPLY, 4, 1), (MULTIPLY, 4, 2), (MULTIPLY, 4, 3), (A_FORWARD, 5, 1, 3), (MULTIPLY, 5, 0), (MULTIPLY, 5, 1),
+    (MULTIPLY, 1, 3), (MULTIPLY, 2, 3), (MULTIPLY, 3, 3), (A_FORWARD, 5, 1, 3), (FINISH, 0), (A_FORWARD, 4, 0, 3),
+    (MULTIPLY, 4, 0), (MULTIPLY, 4, 1), (MULTIPLY, 4, 2), (MULTIPLY, 4, 3), (MULTIPLY, 5, 0), (MULTIPLY, 5, 1),
     (MULTIPLY, 5, 2), (MULTIPLY, 5, 3), (FINISH, 1), (FINISH, 2), (FINISH, 3), (FINISH, 4), (FINISH, 5),
 )
 

time: 60.3 us -> 59.5 us (0.987); the launches traced: 60.2 us -> 58.4 us
  Pallas kernels: 59.4 us -> 57.6 us
    pallas_call x1, Pallas kernels: 59.4 us -> 57.6 us  [on_device(): pl.pallas_call(functools.partial(kernel, ny, nz), out_shape=pltpu.VMEM((t...]
where the time goes in v4:
time: 59.5 us; the launch traced here: 58.4 us
  Pallas kernels  57.6 us (97%)
  local copies, waits for them, and re-layouts  0.75 us (1%)
    pallas_call x1, Pallas kernels, on_device(): pl.pallas_call(functools.partial(kernel, ny, nz), out_shape=pltpu.VMEM((t...  57.6 us

profile of v4, /device:TPU:1, one launch (start us, length us, event | category | flops | bytes accessed | tf_op | source)
XLA Modules:
  0.0 58.4 jit_solution(3593623617524299453)
XLA Ops:
  0.0 57.6 %shard_map.82 = bf16[768,256]{1,0:T(8,128)(2,1)S(1)} custom-call(bf16[768,256]{1,0:T(8,128)(2,1)} %q_hbm.1, bf16[768,256]{1,0:T(8,128)(2,1)} %k_hbm.1, bf16[768,256]{1,0:T(8,128)(2,1)} %v_hbm.1, bf16[127,256]{1,0:T(8,128)(2,1)} %e_hbm.1, f32[256,128]{1,0:T(8,128)} %t_hbm.1, f32[1,256]{1,0:T(1,128)} %bitcast.2, bf16[512,256]{1,0:T(8,128)(2,1)} %w_hbm.1, ...), custom_call_target="tpu_custom_call" | custom-call | flops 3221225472 | bytes 1572864 | tf_op jit(solution)/shard_map/pallas_call | solution.py:385
  57.7 0.7 %copy.10 = bf16[768,256]{1,0:T(8,128)(2,1)} copy(bf16[768,256]{1,0:T(8,128)(2,1)S(1)} %shard_map.82) | data formatting | bytes 786432

commit v5 on v4

--- a/solution.py
+++ b/solution.py
@@ -287,7 +287,7 @@
             src_ref=block,
             dst_ref=block,
             send_sem=m_send_sem,
-            recv_sem=m_recv_sem.at[p, owner],
+            recv_sem=m_recv_sem.at[p],
             device_id=sibling,
             device_id_type=MESH,
         ).start()
@@ -311,9 +311,8 @@
         to_sibling(p, owner)
 
     def b_whole(p):
-        for owner in range(ny):
-            block = b_block(p, owner, 1 - c)
-            pltpu.make_async_copy(block, block, m_recv_sem.at[p, owner]).wait()
+        blocks = b_buf.at[piece_column(p), pl.ds(0, ny * half), :]
+        pltpu.make_async_copy(blocks, blocks, m_recv_sem.at[p]).wait()
 
     def multiply(i, p):
         rows = pl.ds(order[i] * ROWS, ROWS)
@@ -412,7 +411,7 @@
             dma,
             dma((X, 2, ny // 2)),
             dma,
-            dma((X, ny)),
+            dma((X,)),
             dma((2, CORES)),
             dma((X,)),
             dma,

time: 59.5 us -> 59.2 us (level)
  no operation moved by 1% of the time
where the time goes in v5:
time: 59.2 us; the launch traced here: 58.1 us
  Pallas kernels  57.4 us (97%)
  local copies, waits for them, and re-layouts  0.75 us (1%)
    pallas_call x1, Pallas kernels, on_device(): pl.pallas_call(functools.partial(kernel, ny, nz), out_shape=pltpu.VMEM((t...  57.4 us

profile of v5, /device:TPU:1, one launch (start us, length us, event | category | flops | bytes accessed | tf_op | source)
XLA Modules:
  0.0 58.1 jit_solution(5222552131869422923)
XLA Ops:
  0.0 57.4 %shard_map.82 = bf16[768,256]{1,0:T(8,128)(2,1)S(1)} custom-call(bf16[768,256]{1,0:T(8,128)(2,1)} %q_hbm.1, bf16[768,256]{1,0:T(8,128)(2,1)} %k_hbm.1, bf16[768,256]{1,0:T(8,128)(2,1)} %v_hbm.1, bf16[127,256]{1,0:T(8,128)(2,1)} %e_hbm.1, f32[256,128]{1,0:T(8,128)} %t_hbm.1, f32[1,256]{1,0:T(1,128)} %bitcast.2, bf16[512,256]{1,0:T(8,128)(2,1)} %w_hbm.1, ...), custom_call_target="tpu_custom_call" | custom-call | flops 3221225472 | bytes 1572864 | tf_op jit(solution)/shard_map/pallas_call | solution.py:384
  57.4 0.7 %copy.10 = bf16[768,256]{1,0:T(8,128)(2,1)} copy(bf16[768,256]{1,0:T(8,128)(2,1)S(1)} %shard_map.82) | data formatting | bytes 786432
